TPU v7x, 32 devices: a whole 2x2x4 slice. The times are simulated.
32 devices in a mesh: groups: 2 (over x), section: 16 (over z, y, core).
Axes of the slice: x: 2, y: 2, z: 4, core: 2. Of those that a mesh axis runs over, the one named last changes fastest.
Arguments:
- query_grads: bfloat16 [512, 8192], P(('groups', 'section')), parts along dimension 0, may hold values from -8 to 8
- key_vals: bfloat16 [4096, 8192], P(('groups', 'section')), parts along dimension 0, may hold values from -8 to 8
Outputs:
- target_out: bfloat16 [512, 8192], P(('groups', 'section')), parts along dimension 0
- source_grads: bfloat16 [4096, 8192], P(('groups', 'section')), parts along dimension 0
There are 2 independent parts, one for each index of `groups`. A program takes and returns all parts, laid end to end along the dimension named above; each array names one. Nothing has to cross between parts.
All inputs are finite; a program needn't handle non-finite values.
Results may differ from a plain program's by a relative error of at most 0.0052.
Values may be sent and summed in bfloat16 or wider, within the bound.
A program may use at most 128 MiB of HBM per device.

v0:
```python
import math

import jax
import jax.numpy as jnp
from jax import lax
from jax.sharding import PartitionSpec as P

HEAD = 64


def attend_rows(rows_in, keys, vals, width):
    score_scale = width ** (-0.5)
    total = rows_in.shape[0]
    columns = rows_in.shape[1]
    heads_here = columns // (2 * width)
    block = math.gcd(total, 256)
    blocks = rows_in.reshape(total // block, block, heads_here, 2, width)

    def step(carry, pairs):
        query = pairs[:, :, 0]
        dctx = pairs[:, :, 1]
        scores = (
            jnp.einsum("thd,shd->hts", query, keys, preferred_element_type=jnp.float32)
            * score_scale
        )
        probs = jax.nn.softmax(scores, axis=-1)
        probs_low = probs.astype(jnp.bfloat16)
        context = jnp.einsum(
            "hts,shd->thd", probs_low, vals, preferred_element_type=jnp.float32
        ).astype(jnp.bfloat16)
        d_probs = jnp.einsum("thd,shd->hts", dctx, vals, preferred_element_type=jnp.float32)
        d_scores = (
            probs * (d_probs - jnp.sum(probs * d_probs, axis=-1, keepdims=True)) * score_scale
        ).astype(jnp.bfloat16)
        d_query = jnp.einsum(
            "hts,shd->thd", d_scores, keys, preferred_element_type=jnp.float32
        ).astype(jnp.bfloat16)
        key_part = jnp.einsum("hts,thd->shd", d_scores, query, preferred_element_type=jnp.float32)
        value_part = jnp.einsum("hts,thd->shd", probs_low, dctx, preferred_element_type=jnp.float32)
        carry = carry + jnp.stack([key_part, value_part], axis=2)
        out_rows = jnp.stack([context, d_query], axis=2).reshape(block, columns)
        return (carry, out_rows)

    start = jnp.zeros((keys.shape[0], heads_here, 2, width), jnp.float32)
    grads, outs = lax.scan(step, start, blocks)
    return (outs.reshape(total, columns), grads)


def per_device(query_grads, key_vals):
    width = HEAD
    relayed = lax.all_to_all(key_vals, "section", split_axis=1, concat_axis=0, tiled=True)
    src_all = relayed.shape[0]
    columns = relayed.shape[1]
    source_pairs = relayed.reshape(src_all, columns // (2 * width), 2, width)
    keys = source_pairs[:, :, 0]
    vals = source_pairs[:, :, 1]
    gathered = lax.all_to_all(query_grads, "section", split_axis=1, concat_axis=0, tiled=True)
    out_rows, grads = attend_rows(gathered, keys, vals, width)
    target_out = lax.all_to_all(out_rows, "section", split_axis=0, concat_axis=1, tiled=True)
    grads_low = grads.astype(jnp.bfloat16).reshape(src_all, columns)
    source_grads = lax.all_to_all(grads_low, "section", split_axis=0, concat_axis=1, tiled=True)
    return (target_out, source_grads)


def solution(mesh):
    return jax.shard_map(
        per_device,
        mesh=mesh,
        in_specs=(P(("groups", "section"), None), P(("groups", "section"), None)),
        out_specs=(P(("groups", "section"), None), P(("groups", "section"), None)),
        check_vma=False,
    )
```

profile of v0, /device:TPU:13, one launch (start us, length us, event | category | flops | bytes accessed | tf_op | source)
XLA Modules:
  0.0 197.1 jit_solution(2019538392445757520)
XLA Ops:
  0.6 1.7 copy.43
  2.3 6.6 %all-to-all-start = ((bf16[16,16,512]{2,0,1:T(8,128)(2,1)}), bf16[16,16,512]{2,0,1:T(8,128)(2,1)S(1)}, u32[]{:S(2)}, u32[]{:S(2)}) async-start(bf16[16,16,512]{2,0,1:T(8,128)(2,1)} %bitcast.58), calls=%async_computation | async-start | bytes 524288 | tf_op jit(solution)/shard_map/all_to_all | solution.py:57
  8.9 4.1 %copy.25 = bf16[128,8192]{0,1:T(8,128)(2,1)} copy(bf16[128,8192]{1,0:T(8,128)(2,1)} %param.3) | data formatting | bytes 4194304 | tf_op args[1]
  12.9 3.9 %all-to-all-done = bf16[16,16,512]{2,0,1:T(8,128)(2,1)S(1)} async-done(((bf16[16,16,512]{2,0,1:T(8,128)(2,1)}), bf16[16,16,512]{2,0,1:T(8,128)(2,1)S(1)}, u32[]{:S(2)}, u32[]{:S(2)}) %all-to-all-start) | async-done | bytes 262176 | tf_op jit(solution)/shard_map/all_to_all | solution.py:57
  16.8 5.7 %all-to-all-start.1 = ((bf16[128,16,512]{0,2,1:T(8,128)(2,1)}), bf16[128,16,512]{0,2,1:T(8,128)(2,1)S(1)}, u32[]{:S(2)}, u32[]{:S(2)}) async-start(bf16[128,16,512]{0,2,1:T(8,128)(2,1)} %bitcast.2), calls=%async_computation.1 | async-start | bytes 4194304 | tf_op jit(solution)/shard_map/all_to_all | solution.py:51
  22.8 1.5 fusion.56
  24.3 1.2 copy.35
  26.0 44.0 %all-to-all-done.1 = bf16[128,16,512]{0,2,1:T(8,128)(2,1)S(1)} async-done(((bf16[128,16,512]{0,2,1:T(8,128)(2,1)}), bf16[128,16,512]{0,2,1:T(8,128)(2,1)S(1)}, u32[]{:S(2)}, u32[]{:S(2)}) %all-to-all-start.1) | async-done | bytes 2097184 | tf_op jit(solution)/shard_map/all_to_all | solution.py:51
  70.0 2.7 %copy.26 = bf16[16,128,512]{1,0,2:T(8,128)(2,1)} copy(bf16[16,128,512]{1,2,0:T(8,128)(2,1)S(1)} %bitcast.59) | data formatting | bytes 4194304 | tf_op jit(solution)/shard_map/all_to_all | solution.py:51
  72.7 2.8 %reshape.36 = bf16[2048,4,2,64]{0,3,2,1:T(8,128)(2,1)S(1)} reshape(bf16[16,128,512]{1,0,2:T(8,128)(2,1)} %copy.26) | data formatting | bytes 4194304 | tf_op jit(solution)/shard_map/reshape | solution.py:54
  75.5 1.3 fusion.37
  76.8 4.6 %fusion.57 = (f32[4,256]{1,0:T(4,128)S(1)}, f32[4,256,2048]{2,1,0:T(8,128)}) fusion(f32[4,256,2048]{2,1,0:T(8,128)S(1)} %fusion.37), kind=kOutput, calls=%fused_computation.40 | output fusion | flops 8390655 | bytes 16781312 | tf_op jit(solution)/shard_map/while/body/eval_jaxpr/sub | solution.py:26
  81.4 1.1 copy-done
  82.5 4.5 %fusion.38 = f32[4,256,2048]{2,1,0:T(8,128)} fusion(bf16[2048,4,2,64]{0,3,2,1:T(8,128)(2,1)S(1)} %reshape.36, bf16[256,4,1,64]{0,3,1,2:T(8,128)(2,1)S(1)} %copy.38), kind=kOutput, calls=%fused_computation.27 | convolution fusion | flops 268435456 | bytes 9568256 | tf_op jit(solution)/shard_map/while/body/eval_jaxpr/thd,shd->hts/dot_general | solution.py:31
  87.0 8.3 %fusion.34 = bf16[256,4,1,64]{0,3,1,2:T(8,128)(2,1)S(1)} fusion(bf16[2048,4,2,64]{0,3,2,1:T(8,128)(2,1)S(1)} %reshape.36, f32[4,256]{1,0:T(4,128)S(1)} %get-tuple-element.26, f32[4,256,2048]{2,1,0:T(8,128)} %copy-done), kind=kOutput, calls=%fused_computation.23 | convolution fusion | flops 278989824 | bytes 17960960 | tf_op jit(solution)/shard_map/while/body/eval_jaxpr/hts,shd->thd/dot_general | solution.py:28
  95.3 14.0 %fusion.31 = bf16[256,4,1,64]{0,3,1,2:T(8,128)(2,1)S(1)} fusion(f32[4,256,2048]{2,1,0:T(8,128)} %fusion.38, bf16[2048,4,2,64]{0,3,2,1:T(8,128)(2,1)S(1)} %reshape.36, f32[4,256,2048]{2,1,0:T(8,128)} %get-tuple-element.27, f32[4,256]{1,0:T(4,128)S(1)} %get-tuple-element.26), kind=kOutput, calls=%fused_computation.22 | convolution fusion | flops 283184128 | bytes 34742272 | tf_op jit(solution)/shard_map/while/body/eval_jaxpr/hts,shd->thd/dot_general | solution.py:35
  109.8 1.0 all_to_all.56
  110.9 4.9 %all-to-all-start.2 = ((bf16[16,16,512]{2,1,0:T(8,128)(2,1)}), bf16[16,16,512]{2,1,0:T(8,128)(2,1)S(1)}, u32[]{:S(2)}, u32[]{:S(2)}) async-start(bf16[16,16,512]{2,1,0:T(8,128)(2,1)} %all_to_all.56), calls=%async_computation.2 | async-start | bytes 524288 | tf_op jit(solution)/shard_map/all_to_all | solution.py:59
  115.8 8.5 %fusion.21 = bf16[2048,4,1,64]{0,3,1,2:T(8,128)(2,1)S(1)} fusion(bf16[256,4,1,64]{0,3,1,2:T(8,128)(2,1)S(1)} %copy.38, f32[4,256]{1,0:T(4,128)S(1)} %get-tuple-element.26, f32[4,256,2048]{2,1,0:T(8,128)} %copy-done), kind=kOutput, calls=%fused_computation.15 | convolution fusion | flops 279448576 | bytes 9572352 | tf_op jit(solution)/shard_map/while/body/eval_jaxpr/hts,thd->shd/dot_general | solution.py:39
  124.2 13.5 %fusion.18 = bf16[2048,4,1,64]{0,3,1,2:T(8,128)(2,1)S(1)} fusion(f32[4,256,2048]{2,1,0:T(8,128)} %fusion.38, bf16[256,4,1,64]{0,3,1,2:T(8,128)(2,1)S(1)} %copy.35, f32[4,256,2048]{2,1,0:T(8,128)} %get-tuple-element.27, f32[4,256]{1,0:T(4,128)S(1)} %get-tuple-element.26), kind=kOutput, calls=%fused_computation.14 | convolution fusion | flops 283642880 | bytes 17960960 | tf_op jit(solution)/shard_map/while/body/eval_jaxpr/hts,thd->shd/dot_general | solution.py:38
  138.9 1.9 copy.33
  140.8 6.0 %all-to-all-start.3 = ((bf16[16,128,512]{1,2,0:T(8,128)(2,1)}), bf16[16,128,512]{1,2,0:T(8,128)(2,1)S(1)}, u32[]{:S(2)}, u32[]{:S(2)}) async-start(bf16[16,128,512]{1,2,0:T(8,128)(2,1)} %copy.33), calls=%async_computation.3 | async-start | bytes 4194304 | tf_op jit(solution)/shard_map/all_to_all | solution.py:61
  147.5 46.7 %all-to-all-done.3 = bf16[16,128,512]{1,2,0:T(8,128)(2,1)S(1)} async-done(((bf16[16,128,512]{1,2,0:T(8,128)(2,1)}), bf16[16,128,512]{1,2,0:T(8,128)(2,1)S(1)}, u32[]{:S(2)}, u32[]{:S(2)}) %all-to-all-start.3) | async-done | bytes 2097184 | tf_op jit(solution)/shard_map/all_to_all | solution.py:61
  194.2 2.9 %copy.34 = bf16[128,8192]{1,0:T(8,128)(2,1)} copy(bf16[128,8192]{0,1:T(8,128)(2,1)S(1)} %bitcast.60) | data formatting | bytes 4194304
  (10 shorter events, 3.0 us)
Async XLA Ops:
  2.3 14.5 %all-to-all-start = ((bf16[16,16,512]{2,0,1:T(8,128)(2,1)}), bf16[16,16,512]{2,0,1:T(8,128)(2,1)S(1)}, u32[]{:S(2)}, u32[]{:S(2)}) async-start(bf16[16,16,512]{2,0,1:T(8,128)(2,1)} %bitcast.58), calls=%async_computation | async-start | bytes 524288 | tf_op jit(solution)/shard_map/all_to_all | solution.py:57
  16.8 53.2 %all-to-all-start.1 = ((bf16[128,16,512]{0,2,1:T(8,128)(2,1)}), bf16[128,16,512]{0,2,1:T(8,128)(2,1)S(1)}, u32[]{:S(2)}, u32[]{:S(2)}) async-start(bf16[128,16,512]{0,2,1:T(8,128)(2,1)} %bitcast.2), calls=%async_computation.1 | async-start | bytes 4194304 | tf_op jit(solution)/shard_map/all_to_all | solution.py:51
  76.8 5.7 %copy-start = (f32[4,256,2048]{2,1,0:T(8,128)}, f32[4,256,2048]{2,1,0:T(8,128)S(1)}, u32[]{:S(2)}) copy-start(f32[4,256,2048]{2,1,0:T(8,128)S(1)} %fusion.37) | copy-start | bytes 25165828
  110.9 29.9 %all-to-all-start.2 = ((bf16[16,16,512]{2,1,0:T(8,128)(2,1)}), bf16[16,16,512]{2,1,0:T(8,128)(2,1)S(1)}, u32[]{:S(2)}, u32[]{:S(2)}) async-start(bf16[16,16,512]{2,1,0:T(8,128)(2,1)} %all_to_all.56), calls=%async_computation.2 | async-start | bytes 524288 | tf_op jit(solution)/shard_map/all_to_all | solution.py:59
  140.8 53.4 %all-to-all-start.3 = ((bf16[16,128,512]{1,2,0:T(8,128)(2,1)}), bf16[16,128,512]{1,2,0:T(8,128)(2,1)S(1)}, u32[]{:S(2)}, u32[]{:S(2)}) async-start(bf16[16,128,512]{1,2,0:T(8,128)(2,1)} %copy.33), calls=%async_computation.3 | async-start | bytes 4194304 | tf_op jit(solution)/shard_map/all_to_all | solution.py:61
where the time goes:
time: 198 us; the launch traced here: 197 us
  waiting for transfers between devices  94.6 us (48%)
  matrix products  50.2 us (25%)
  local copies, waits for them, and re-layouts  23.6 us (12%)
  starting transfers between devices  23.2 us (12%)
  other arithmetic  4.79 us (2%)
    all_to_all x1, waiting for transfers between devices, per_device(): lax.all_to_all(grads_low, 'section', split_axis=0, concat_axis=1, tiled=T...  46.7 us
    all_to_all x1, waiting for transfers between devices, per_device(): lax.all_to_all(key_vals, 'section', split_axis=1, concat_axis=0, tiled=True)  44 us
    dot_general x1, matrix products, step(): jnp.einsum('hts,shd->thd', d_scores, keys, preferred_element_type=jnp.flo...  14 us
    dot_general x1, matrix products, step(): jnp.einsum('hts,thd->shd', d_scores, query, preferred_element_type=jnp.fl...  13.5 us
    unnamed x7, local copies, waits for them, and re-layouts  10.4 us
    dot_general x1, matrix products, step(): jnp.einsum('hts,thd->shd', probs_low, dctx, preferred_element_type=jnp.fl...  8.5 us
    dot_general x1, matrix products, step(): jnp.einsum('hts,shd->thd', probs_low, vals, preferred_element_type=jnp.fl...  8.33 us
    all_to_all x1, starting transfers between devices, per_device(): lax.all_to_all(query_grads, 'section', split_axis=1, concat_axis=0, tiled...  6.55 us
  transfers between devices with their start and end apart: 4, of which 3 were waited for; matrix products, arithmetic and copies ran while one was open for 17% of the time, Pallas kernels for 0%

commit v1 on v0

v1 whole, which is shorter than its diff:
```python
import math

import jax
import jax.numpy as jnp
from jax import lax
from jax.experimental import pallas as pl
from jax.experimental.pallas import tpu as pltpu
from jax.sharding import PartitionSpec as P

HEAD = 64
PAIR = 2 * HEAD
CHUNKS = 1


def dot(a, b, da, db):
    return lax.dot_general(
        a, b, (((da,), (db,)), ((), ())), preferred_element_type=jnp.float32
    )


def attend(scale, step, qd_ref, kv_ref, out_ref, sg_ref, s_scr, dp_scr, acc):
    sources = kv_ref.shape[0]
    targets = qd_ref.shape[0]
    steps = sources // step
    block = pl.program_id(1)
    blocks = pl.num_programs(1)
    qd = qd_ref[...]
    lane = lax.broadcasted_iota(jnp.int32, (step, PAIR), 1)
    first = lane < HEAD
    zero = jnp.zeros((step, PAIR), jnp.bfloat16)
    low = jnp.full((8, targets), -jnp.inf, jnp.float32)

    peak = low
    for i in range(steps):
        rows = pl.ds(i * step, step)
        kv = kv_ref[rows, :]
        s = dot(jnp.where(first, kv, zero), qd, 1, 1) * scale
        s_scr[rows, :] = s
        dp_scr[rows, :] = dot(jnp.where(first, zero, kv), qd, 1, 1)
        peak = jnp.maximum(peak, jnp.max(s.reshape(step // 8, 8, targets), axis=0))
    peak = jnp.max(peak, axis=0, keepdims=True)

    total = jnp.zeros((8, targets), jnp.float32)
    mixed = jnp.zeros((8, targets), jnp.float32)
    for i in range(steps):
        rows = pl.ds(i * step, step)
        e = jnp.exp(s_scr[rows, :] - peak)
        s_scr[rows, :] = e
        total = total + jnp.sum(e.reshape(step // 8, 8, targets), axis=0)
        mixed = mixed + jnp.sum((e * dp_scr[rows, :]).reshape(step // 8, 8, targets), axis=0)
    inverse = 1.0 / jnp.sum(total, axis=0, keepdims=True)
    shift = jnp.sum(mixed, axis=0, keepdims=True) * inverse

    out = jnp.zeros((targets, PAIR), jnp.float32)
    for i in range(steps):
        rows = pl.ds(i * step, step)
        probs = s_scr[rows, :] * inverse
        probs_low = probs.astype(jnp.bfloat16)
        d_scores = (probs * (dp_scr[rows, :] - shift) * scale).astype(jnp.bfloat16)
        kv = kv_ref[rows, :]
        vk = jnp.concatenate([kv[:, HEAD:], kv[:, :HEAD]], axis=1)
        out = out + dot(probs_low, jnp.where(first, vk, zero), 0, 0)
        out = out + dot(d_scores, jnp.where(first, zero, vk), 0, 0)
        grads = jnp.where(first, dot(d_scores, qd, 1, 0), dot(probs_low, qd, 1, 0))
        if acc is None:
            sg_ref[rows, :] = grads.astype(jnp.bfloat16)
        else:
            prior = jnp.where(block == 0, 0.0, acc[rows, :])
            grads = prior + grads
            acc[rows, :] = grads

            @pl.when(block == blocks - 1)
            def _():
                sg_ref[rows, :] = grads.astype(jnp.bfloat16)

    out_ref[...] = out.astype(jnp.bfloat16)


def attention(qd, kv):
    targets, columns = qd.shape
    sources = kv.shape[0]
    heads = columns // PAIR
    tile = math.gcd(targets, 256)
    step = math.gcd(sources, 256)
    scale = HEAD ** (-0.5)
    single = targets == tile
    scratch = [
        pltpu.VMEM((sources, tile), jnp.float32),
        pltpu.VMEM((sources, tile), jnp.float32),
    ]
    if single:
        def body(*refs):
            attend(scale, step, *refs, None)
    else:
        scratch.append(pltpu.VMEM((sources, PAIR), jnp.float32))

        def body(*refs):
            attend(scale, step, *refs)

    return pl.pallas_call(
        body,
        grid=(heads, targets // tile),
        out_shape=(
            jax.ShapeDtypeStruct((targets, columns), jnp.bfloat16),
            jax.ShapeDtypeStruct((sources, columns), jnp.bfloat16),
        ),
        in_specs=[
            pl.BlockSpec((tile, PAIR), lambda h, t: (t, h)),
            pl.BlockSpec((sources, PAIR), lambda h, t: (0, h)),
        ],
        out_specs=(
            pl.BlockSpec((tile, PAIR), lambda h, t: (t, h)),
            pl.BlockSpec((sources, PAIR), lambda h, t: (0, h)),
        ),
        scratch_shapes=scratch,
        compiler_params=pltpu.CompilerParams(vmem_limit_bytes=48 * 1024 * 1024),
        cost_estimate=pl.CostEstimate(
            flops=24 * targets * sources * PAIR * heads,
            bytes_accessed=4 * (targets + sources) * columns,
            transcendentals=targets * sources * heads,
        ),
        name="attention",
    )(qd, kv)


def to_heads(x):
    return lax.all_to_all(x, "section", split_axis=1, concat_axis=0, tiled=True)


def to_rows(x):
    return lax.all_to_all(x, "section", split_axis=0, concat_axis=1, tiled=True)


def solution(mesh):
    devices = mesh.shape["section"]

    def per_device(query_grads, key_vals):
        columns = query_grads.shape[1]
        chunks = math.gcd(CHUNKS, columns // (PAIR * devices))
        width = columns // chunks
        outs, grads = [], []
        for c in range(chunks):
            part = slice(c * width, (c + 1) * width)
            qd = to_heads(query_grads[:, part])
            kv = to_heads(key_vals[:, part])
            out, grad = attention(qd, kv)
            outs.append(to_rows(out))
            grads.append(to_rows(grad))
        return jnp.concatenate(outs, axis=1), jnp.concatenate(grads, axis=1)

    return jax.shard_map(
        per_device,
        mesh=mesh,
        in_specs=(P(("groups", "section"), None), P(("groups", "section"), None)),
        out_specs=(P(("groups", "section"), None), P(("groups", "section"), None)),
        check_vma=False,
    )
```

time: 198 us -> 150 us (0.76)
  blocking collectives: 0 us -> 65 us
  matrix products: 50.2 us -> 0 us
  waiting for transfers between devices: 94.6 us -> 52.9 us
  local copies, waits for them, and re-layouts: 23.6 us -> 5.75 us
  Pallas kernels: 0 us -> 12.9 us
  starting transfers between devices: 23.2 us -> 12.3 us
  other arithmetic: 4.79 us -> 0 us
    all_to_all x0 -> x2, blocking collectives: none -> 65 us  [the longest x1 52.2 us: to_heads(): return lax.all_to_all(x, 'section', split_axis=1, concat_axis=0, tiled=True)]
    dot_general x6 -> x0, matrix products: 50.2 us -> none  [the longest x1 14 us: step(): jnp.einsum('hts,shd->thd', d_scores, keys, preferred_element_type=jnp.flo...]
    all_to_all x4 -> x2, waiting for transfers between devices: 94.6 us -> 52.9 us  [the longest x1 46.7 us: to_rows(): return lax.all_to_all(x, 'section', split_axis=0, concat_axis=1, tiled=True)]
    pallas_call x0 -> x1, Pallas kernels: none -> 12.9 us  [attention(): pl.pallas_call(body, grid=(heads, targets // tile), out_shape=(jax.ShapeD...]
    all_to_all x4 -> x2, starting transfers between devices: 23.2 us -> 12.3 us  [the longest x1 6.55 us: to_heads(): return lax.all_to_all(x, 'section', split_axis=1, concat_axis=0, tiled=True)]
    unnamed x7 -> x0, local copies, waits for them, and re-layouts: 10.4 us -> none
    sub x1 -> x0, other arithmetic: 4.57 us -> none  [step(): probs = jax.nn.softmax(scores, axis=-1)]
    reshape x1 -> x0, local copies, waits for them, and re-layouts: 2.82 us -> none  [per_device(): source_pairs = relayed.reshape(src_all, columns // (2 * width), 2, width)]
  transfers between devices with their start and end apart: 4 -> 2, of which waited for: 3 -> 2; matrix products, arithmetic and copies ran while one was open for 17% -> 2% of each run, Pallas kernels for 0% -> 0%
where the time goes in v1:
time: 150 us; the launch traced here: 149 us
  blocking collectives  65 us (43%)
  waiting for transfers between devices  52.9 us (35%)
  Pallas kernels  12.9 us (9%)
  starting transfers between devices  12.3 us (8%)
  local copies, waits for them, and re-layouts  5.75 us (4%)
    all_to_all x1, blocking collectives, to_heads(): return lax.all_to_all(x, 'section', split_axis=1, concat_axis=0, tiled=True)  52.2 us
    all_to_all x1, waiting for transfers between devices, to_rows(): return lax.all_to_all(x, 'section', split_axis=0, concat_axis=1, tiled=True)  46.7 us
    pallas_call x1, Pallas kernels, attention(): pl.pallas_call(body, grid=(heads, targets // tile), out_shape=(jax.ShapeD...  12.9 us
    all_to_all x1, blocking collectives, to_rows(): return lax.all_to_all(x, 'section', split_axis=0, concat_axis=1, tiled=True)  12.9 us
    all_to_all x1, starting transfers between devices, to_heads(): return lax.all_to_all(x, 'section', split_axis=1, concat_axis=0, tiled=True)  6.55 us
    all_to_all x1, waiting for transfers between devices, to_heads(): return lax.all_to_all(x, 'section', split_axis=1, concat_axis=0, tiled=True)  6.14 us
    all_to_all x1, starting transfers between devices, to_rows(): return lax.all_to_all(x, 'section', split_axis=0, concat_axis=1, tiled=True)  5.73 us
    all_to_all x2, local copies, waits for them, and re-layouts, to_heads(): return lax.all_to_all(x, 'section', split_axis=1, concat_axis=0, tiled=True)  3.49 us
  transfers between devices with their start and end apart: 2, of which 2 were waited for; matrix products, arithmetic and copies ran while one was open for 2% of the time, Pallas kernels for 0%

profile of v1, /device:TPU:13, one launch (start us, length us, event | category | flops | bytes accessed | tf_op | source)
XLA Modules:
  0.0 149.5 jit_solution(1423340175162589953)
XLA Ops:
  0.6 1.7 %copy.15 = bf16[2,16,8,512]{3,2,0,1:T(8,128)(2,1)} copy(bf16[2,16,8,512]{3,2,1,0:T(8,128)(2,1)} %bitcast.30) | data formatting | bytes 524288 | tf_op jit(solution)/shard_map/all_to_all | solution.py:127
  2.3 6.6 %all-to-all-start = ((bf16[16,16,512]{2,0,1:T(8,128)(2,1)}), bf16[16,16,512]{2,0,1:T(8,128)(2,1)S(1)}, u32[]{:S(2)}, u32[]{:S(2)}) async-start(bf16[16,16,512]{2,0,1:T(8,128)(2,1)} %bitcast.21), calls=%async_computation | async-start | bytes 524288 | tf_op jit(solution)/shard_map/all_to_all | solution.py:127
  8.9 1.8 %copy.14 = bf16[16,16,8,512]{3,2,0,1:T(8,128)(2,1)S(1)} copy(bf16[16,16,8,512]{3,2,1,0:T(8,128)(2,1)} %bitcast.27) | data formatting | bytes 4194304 | tf_op jit(solution)/shard_map/all_to_all | solution.py:127
  10.7 6.1 %all-to-all-done = bf16[16,16,512]{2,0,1:T(8,128)(2,1)S(1)} async-done(((bf16[16,16,512]{2,0,1:T(8,128)(2,1)}), bf16[16,16,512]{2,0,1:T(8,128)(2,1)S(1)}, u32[]{:S(2)}, u32[]{:S(2)}) %all-to-all-start) | async-done | bytes 262176 | tf_op jit(solution)/shard_map/all_to_all | solution.py:127
  16.8 52.2 %all_to_all.76 = bf16[128,16,512]{2,0,1:T(8,128)(2,1)S(1)} all-to-all(bf16[128,16,512]{2,0,1:T(8,128)(2,1)S(1)} %bitcast.26), channel_id=1, replica_groups=mesh['groups'=2,'section'=16] {'section'}, dimensions={1} | all-to-all | bytes 4194304 | tf_op jit(solution)/shard_map/all_to_all | solution.py:127
  69.0 12.9 %attention.1 = (bf16[256,512]{1,0:T(8,128)(2,1)S(1)}, bf16[2048,512]{1,0:T(8,128)(2,1)}) custom-call(bf16[256,512]{1,0:T(8,128)(2,1)S(1)} %bitcast.23, bf16[2048,512]{1,0:T(8,128)(2,1)S(1)} %bitcast.22), custom_call_target="tpu_custom_call" | custom-call | flops 6442450944 | bytes 4718592 | tf_op jit(solution)/shard_map/attention/pallas_call | solution.py:100
  81.9 12.9 %all_to_all.77 = bf16[16,16,512]{2,1,0:T(8,128)(2,1)S(1)} all-to-all(bf16[16,16,512]{2,1,0:T(8,128)(2,1)S(1)} %bitcast.24), channel_id=1, replica_groups=mesh['groups'=2,'section'=16] {'section'}, dimensions={0} | all-to-all | bytes 524288 | tf_op jit(solution)/shard_map/all_to_all | solution.py:131
  94.7 5.7 %all-to-all-start.3 = ((bf16[16,128,512]{2,1,0:T(8,128)(2,1)}), bf16[16,128,512]{2,1,0:T(8,128)(2,1)S(1)}, u32[]{:S(2)}, u32[]{:S(2)}) async-start(bf16[16,128,512]{2,1,0:T(8,128)(2,1)} %bitcast.6), calls=%async_computation.3 | async-start | bytes 4194304 | tf_op jit(solution)/shard_map/all_to_all | solution.py:131
  100.5 0.7 copy.10
  101.2 46.7 %all-to-all-done.3 = bf16[16,128,512]{2,1,0:T(8,128)(2,1)S(1)} async-done(((bf16[16,128,512]{2,1,0:T(8,128)(2,1)}), bf16[16,128,512]{2,1,0:T(8,128)(2,1)S(1)}, u32[]{:S(2)}, u32[]{:S(2)}) %all-to-all-start.3) | async-done | bytes 2097184 | tf_op jit(solution)/shard_map/all_to_all | solution.py:131
  147.9 1.5 %copy.11 = bf16[16,16,8,512]{3,2,0,1:T(8,128)(2,1)} copy(bf16[16,16,8,512]{3,2,1,0:T(8,128)(2,1)S(1)} %bitcast.25) | data formatting | bytes 4194304 | tf_op jit(solution)/shard_map/all_to_all | solution.py:131
Async XLA Ops:
  2.3 14.5 %all-to-all-start = ((bf16[16,16,512]{2,0,1:T(8,128)(2,1)}), bf16[16,16,512]{2,0,1:T(8,128)(2,1)S(1)}, u32[]{:S(2)}, u32[]{:S(2)}) async-start(bf16[16,16,512]{2,0,1:T(8,128)(2,1)} %bitcast.21), calls=%async_computation | async-start | bytes 524288 | tf_op jit(solution)/shard_map/all_to_all | solution.py:127
  94.7 53.2 %all-to-all-start.3 = ((bf16[16,128,512]{2,1,0:T(8,128)(2,1)}), bf16[16,128,512]{2,1,0:T(8,128)(2,1)S(1)}, u32[]{:S(2)}, u32[]{:S(2)}) async-start(bf16[16,128,512]{2,1,0:T(8,128)(2,1)} %bitcast.6), calls=%async_computation.3 | async-start | bytes 4194304 | tf_op jit(solution)/shard_map/all_to_all | solution.py:131

commit v2 on v0

v2 whole, which is shorter than its diff:
```python
import functools
import math

import jax
import jax.numpy as jnp
from jax import lax
from jax.experimental import pallas as pl
from jax.experimental.pallas import tpu as pltpu
from jax.sharding import PartitionSpec as P

HEAD = 64
PAIR = 2 * HEAD


def dot(a, b, da, db):
    return lax.dot_general(
        a, b, (((da,), (db,)), ((), ())), preferred_element_type=jnp.float32
    )


def attend(h, tile, step, qd_all, kv_all, out_all, sg_all, s_scr, dp_scr, acc):
    scale = HEAD ** (-0.5)
    sources = kv_all.shape[1]
    targets = qd_all.shape[1]
    tiles = targets // tile
    steps = sources // step
    first = lax.broadcasted_iota(jnp.int32, (step, PAIR), 1) < HEAD
    zero = jnp.zeros((step, PAIR), jnp.bfloat16)

    for t in range(tiles):
        qd = qd_all[h, pl.ds(t * tile, tile), :]
        peak = jnp.full((8, tile), -jnp.inf, jnp.float32)
        for i in range(steps):
            rows = pl.ds(i * step, step)
            kv = kv_all[h, rows, :]
            s = dot(jnp.where(first, kv, zero), qd, 1, 1) * scale
            s_scr[rows, :] = s
            dp_scr[rows, :] = dot(jnp.where(first, zero, kv), qd, 1, 1)
            peak = jnp.maximum(peak, jnp.max(s.reshape(step // 8, 8, tile), axis=0))
        peak = jnp.max(peak, axis=0, keepdims=True)

        total = jnp.zeros((8, tile), jnp.float32)
        mixed = jnp.zeros((8, tile), jnp.float32)
        for i in range(steps):
            rows = pl.ds(i * step, step)
            e = jnp.exp(s_scr[rows, :] - peak)
            s_scr[rows, :] = e
            total = total + jnp.sum(e.reshape(step // 8, 8, tile), axis=0)
            mixed = mixed + jnp.sum((e * dp_scr[rows, :]).reshape(step // 8, 8, tile), axis=0)
        inverse = 1.0 / jnp.sum(total, axis=0, keepdims=True)
        shift = jnp.sum(mixed, axis=0, keepdims=True) * inverse

        out = jnp.zeros((tile, PAIR), jnp.float32)
        for i in range(steps):
            rows = pl.ds(i * step, step)
            probs = s_scr[rows, :] * inverse
            probs_low = probs.astype(jnp.bfloat16)
            d_scores = (probs * (dp_scr[rows, :] - shift) * scale).astype(jnp.bfloat16)
            kv = kv_all[h, rows, :]
            vk = jnp.concatenate([kv[:, HEAD:], kv[:, :HEAD]], axis=1)
            out = out + dot(probs_low, jnp.where(first, vk, zero), 0, 0)
            out = out + dot(d_scores, jnp.where(first, zero, vk), 0, 0)
            grads = jnp.where(first, dot(d_scores, qd, 1, 0), dot(probs_low, qd, 1, 0))
            if t > 0:
                grads = acc[rows, :] + grads
            if t < tiles - 1:
                acc[rows, :] = grads
            else:
                sg_all[h, rows, :] = grads.astype(jnp.bfloat16)
        out_all[h, pl.ds(t * tile, tile), :] = out.astype(jnp.bfloat16)


def kernel(
    n, heads, tile, step,
    qg, kvs, to, sg,
    qd_all, kv_all, out_all, sg_all, s_scr, dp_scr, acc,
    q_send, q_recv, k_send, k_recv, o_send, o_recv, g_send, g_recv, own,
):
    me = lax.axis_index("section")
    t_rows = qg.shape[0]
    s_rows = kvs.shape[0]

    def partner(d):
        return lax.rem(me + d, n)

    def rows_of(p, rows):
        return pl.ds(pl.multiple_of(p * rows, rows), rows)

    def cols_of(p, h):
        return pl.ds(pl.multiple_of((p * heads + h) * PAIR, PAIR), PAIR)

    def push(src, dst, send, recv, p):
        return pltpu.make_async_remote_copy(
            src_ref=src, dst_ref=dst, send_sem=send, recv_sem=recv,
            device_id={"section": p}, device_id_type=pl.DeviceIdType.MESH,
        )

    def q_copy(h, p, w):
        return push(qg.at[:, cols_of(p, h)], qd_all.at[h, rows_of(w, t_rows), :],
                    q_send.at[h, p], q_recv.at[h, w], p)

    def k_copy(h, p, w):
        return push(kvs.at[:, cols_of(p, h)], kv_all.at[h, rows_of(w, s_rows), :],
                    k_send.at[h, p], k_recv.at[h, w], p)

    def o_copy(h, p, w):
        return push(out_all.at[h, rows_of(p, t_rows), :], to.at[:, cols_of(w, h)],
                    o_send.at[h, p], o_recv.at[h, w], p)

    def g_copy(h, p, w):
        return push(sg_all.at[h, rows_of(p, s_rows), :], sg.at[:, cols_of(w, h)],
                    g_send.at[h, p], g_recv.at[h, w], p)

    def own_in(h):
        return (
            pltpu.make_async_copy(qg.at[:, cols_of(me, h)], qd_all.at[h, rows_of(me, t_rows), :], own.at[0, h]),
            pltpu.make_async_copy(kvs.at[:, cols_of(me, h)], kv_all.at[h, rows_of(me, s_rows), :], own.at[1, h]),
        )

    def own_out(h):
        return (
            pltpu.make_async_copy(out_all.at[h, rows_of(me, t_rows), :], to.at[:, cols_of(me, h)], own.at[2, h]),
            pltpu.make_async_copy(sg_all.at[h, rows_of(me, s_rows), :], sg.at[:, cols_of(me, h)], own.at[3, h]),
        )

    def each(body):
        @pl.loop(1, n)
        def _(d):
            body(partner(d))

    barrier = pltpu.get_barrier_semaphore()
    each(lambda p: pl.semaphore_signal(
        barrier, inc=1, device_id={"section": p}, device_id_type=pl.DeviceIdType.MESH))

    @pl.loop(0, heads)
    def _(h):
        for c in own_in(h):
            c.start()

    pl.semaphore_wait(barrier, n - 1)

    @pl.loop(0, heads)
    def _(h):
        def send(p):
            q_copy(h, p, me).start()
            k_copy(h, p, me).start()
        each(send)

    @pl.loop(0, heads)
    def _(h):
        for c in own_in(h):
            c.wait()

        def arrive(p):
            q_copy(h, me, p).wait_recv()
            k_copy(h, me, p).wait_recv()
        each(arrive)

        attend(h, tile, step, qd_all, kv_all, out_all, sg_all, s_scr, dp_scr, acc)

        def send(p):
            g_copy(h, p, me).start()
            o_copy(h, p, me).start()
        each(send)
        for c in own_out(h):
            c.start()

    @pl.loop(0, heads)
    def _(h):
        for c in own_out(h):
            c.wait()

        def finish(p):
            q_copy(h, p, me).wait_send()
            k_copy(h, p, me).wait_send()
            o_copy(h, p, me).wait_send()
            g_copy(h, p, me).wait_send()
            o_copy(h, me, p).wait_recv()
            g_copy(h, me, p).wait_recv()
        each(finish)


def solution(mesh):
    n = mesh.shape["section"]

    def per_device(query_grads, key_vals):
        t_rows, columns = query_grads.shape
        s_rows = key_vals.shape[0]
        heads = columns // (PAIR * n)
        targets, sources = t_rows * n, s_rows * n
        tile = math.gcd(targets, 256)
        step = max(math.gcd(sources, 256), sources // 8)
        anywhere = pl.BlockSpec(memory_space=pl.ANY)
        sems = pltpu.SemaphoreType.DMA((heads, n))
        return pl.pallas_call(
            functools.partial(kernel, n, heads, tile, step),
            out_shape=(
                jax.ShapeDtypeStruct(query_grads.shape, jnp.bfloat16),
                jax.ShapeDtypeStruct(key_vals.shape, jnp.bfloat16),
            ),
            in_specs=[anywhere, anywhere],
            out_specs=(anywhere, anywhere),
            scratch_shapes=[
                pltpu.VMEM((heads, targets, PAIR), jnp.bfloat16),
                pltpu.VMEM((heads, sources, PAIR), jnp.bfloat16),
                pltpu.VMEM((heads, targets, PAIR), jnp.bfloat16),
                pltpu.VMEM((heads, sources, PAIR), jnp.bfloat16),
                pltpu.VMEM((sources, tile), jnp.float32),
                pltpu.VMEM((sources, tile), jnp.float32),
                pltpu.VMEM((sources if targets > tile else 8, PAIR), jnp.float32),
            ] + [sems] * 8 + [pltpu.SemaphoreType.DMA((4, heads))],
            compiler_params=pltpu.CompilerParams(
                collective_id=0, has_side_effects=True,
                vmem_limit_bytes=48 * 1024 * 1024,
            ),
            cost_estimate=pl.CostEstimate(
                flops=24 * targets * sources * PAIR * heads,
                bytes_accessed=4 * (targets + sources) * columns // n,
                transcendentals=targets * sources * heads,
            ),
            name="exchange_attention",
        )(query_grads, key_vals)

    return jax.shard_map(
        per_device,
        mesh=mesh,
        in_specs=(P(("groups", "section"), None), P(("groups", "section"), None)),
        out_specs=(P(("groups", "section"), None), P(("groups", "section"), None)),
        check_vma=False,
    )
```

time: 198 us -> 117 us (0.59)
  Pallas kernels: 0 us -> 111 us
  waiting for transfers between devices: 94.6 us -> 0 us
  matrix products: 50.2 us -> 0 us
  starting transfers between devices: 23.2 us -> 0 us
  local copies, waits for them, and re-layouts: 23.6 us -> 4.56 us
  other arithmetic: 4.79 us -> 0 us
    pallas_call x0 -> x1, Pallas kernels: none -> 111 us  [per_device(): pl.pallas_call(functools.partial(kernel, n, heads, tile, step), out_shape...]
    all_to_all x4 -> x0, waiting for transfers between devices: 94.6 us -> none  [the longest x1 46.7 us: per_device(): lax.all_to_all(grads_low, 'section', split_axis=0, concat_axis=1, tiled=T...]
    dot_general x6 -> x0, matrix products: 50.2 us -> none  [the longest x1 14 us: step(): jnp.einsum('hts,shd->thd', d_scores, keys, preferred_element_type=jnp.flo...]
    all_to_all x4 -> x0, starting transfers between devices: 23.2 us -> none  [the longest x1 6.55 us: per_device(): lax.all_to_all(query_grads, 'section', split_axis=1, concat_axis=0, tiled...]
    all_to_all x4 -> x0, local copies, waits for them, and re-layouts: 6.1 us -> none  [the longest x1 2.67 us: per_device(): lax.all_to_all(key_vals, 'section', split_axis=1, concat_axis=0, tiled=True)]
    unnamed x7 -> x6, local copies, waits for them, and re-layouts: 10.4 us -> 4.56 us
    sub x1 -> x0, other arithmetic: 4.57 us -> none  [step(): probs = jax.nn.softmax(scores, axis=-1)]
    reshape x1 -> x0, local copies, waits for them, and re-layouts: 2.82 us -> none  [per_device(): source_pairs = relayed.reshape(src_all, columns // (2 * width), 2, width)]
  transfers between devices with their start and end apart: 4 -> 0, of which waited for: 3 -> 0; matrix products, arithmetic and copies ran while one was open for 17% -> 0% of each run, Pallas kernels for 0% -> 0%
where the time goes in v2:
time: 117 us; the launch traced here: 116 us
  Pallas kernels  111 us (95%)
  local copies, waits for them, and re-layouts  4.56 us (4%)
    pallas_call x1, Pallas kernels, per_device(): pl.pallas_call(functools.partial(kernel, n, heads, tile, step), out_shape...  111 us
    unnamed x6, local copies, waits for them, and re-layouts  4.56 us

profile of v2, /device:TPU:13, one launch (start us, length us, event | category | flops | bytes accessed | tf_op | source)
XLA Modules:
  0.0 116.5 jit_solution(14104890921762524752)
XLA Ops:
  0.6 0.0 copy-start
  0.6 1.6 %copy-done = bf16[128,8192]{1,0:T(8,128)(2,1)S(1)} copy-done((bf16[128,8192]{1,0:T(8,128)(2,1)S(1)}, bf16[128,8192]{1,0:T(8,128)(2,1)}, u32[]{:S(2)}) %copy-start) | copy-done | bytes 2097176
  2.2 0.0 copy-start.1
  2.2 0.9 copy-done.1
  3.2 111.3 %exchange_attention.1 = (bf16[16,8192]{1,0:T(8,128)(2,1)S(1)}, bf16[128,8192]{1,0:T(8,128)(2,1)S(1)}) custom-call(bf16[16,8192]{1,0:T(8,128)(2,1)S(1)} %copy-done.1, bf16[128,8192]{1,0:T(8,128)(2,1)S(1)} %copy-done), custom_call_target="tpu_custom_call" | custom-call | flops 6442450944 | bytes 4718592 | tf_op jit(solution)/shard_map/exchange_attention/pallas_call | solution.py:195
  114.5 0.7 copy.6
  115.2 1.3 %copy.7 = bf16[128,8192]{1,0:T(8,128)(2,1)} copy(bf16[128,8192]{1,0:T(8,128)(2,1)S(1)} %get-tuple-element.5) | data formatting | bytes 4194304
Async XLA Ops:
  0.6 1.6 %copy-start = (bf16[128,8192]{1,0:T(8,128)(2,1)S(1)}, bf16[128,8192]{1,0:T(8,128)(2,1)}, u32[]{:S(2)}) copy-start(bf16[128,8192]{1,0:T(8,128)(2,1)} %kvs.1) | copy-start | bytes 6291460
  2.2 0.9 copy-start.1

commit v3 on v2

v3 whole, which is shorter than its diff:
```python
import functools
import math

import jax
import jax.numpy as jnp
from jax import lax
from jax.experimental import pallas as pl
from jax.experimental.pallas import tpu as pltpu
from jax.sharding import PartitionSpec as P

HEAD = 64
PAIR = 2 * HEAD


def dot(a, b, da, db):
    return lax.dot_general(
        a, b, (((da,), (db,)), ((), ())), preferred_element_type=jnp.float32
    )


def scan_scores(q, kv_head, rows_step, s_out, dp_out, stats):
    scale = HEAD ** (-0.5)
    tile = q.shape[0]
    steps = kv_head.shape[0] // rows_step
    first = lax.broadcasted_iota(jnp.int32, (rows_step, PAIR), 1) < HEAD
    zero = jnp.zeros((rows_step, PAIR), jnp.bfloat16)
    peak = jnp.full((8, tile), -jnp.inf, jnp.float32)
    for i in range(steps):
        rows = pl.ds(i * rows_step, rows_step)
        kv = kv_head[rows, :]
        s = dot(jnp.where(first, kv, zero), q, 1, 1) * scale
        s_out[rows, :] = s
        dp_out[rows, :] = dot(jnp.where(first, zero, kv), q, 1, 1)
        peak = jnp.maximum(peak, jnp.max(s.reshape(rows_step // 8, 8, tile), axis=0))
    peak = jnp.max(peak, axis=0, keepdims=True)
    total = jnp.zeros((8, tile), jnp.float32)
    mixed = jnp.zeros((8, tile), jnp.float32)
    for i in range(steps):
        rows = pl.ds(i * rows_step, rows_step)
        e = jnp.exp(s_out[rows, :] - peak)
        s_out[rows, :] = e
        total = total + jnp.sum(e.reshape(rows_step // 8, 8, tile), axis=0)
        mixed = mixed + jnp.sum((e * dp_out[rows, :]).reshape(rows_step // 8, 8, tile), axis=0)
    total = jnp.sum(total, axis=0, keepdims=True)
    mixed = jnp.sum(mixed, axis=0, keepdims=True)
    stats[...] = jnp.concatenate(
        [peak, total, mixed, jnp.zeros((5, tile), jnp.float32)], axis=0)


def merge(mine, other):
    peak = jnp.maximum(mine[0:1, :], other[0:1, :])
    here = jnp.exp(mine[0:1, :] - peak)
    there = jnp.exp(other[0:1, :] - peak)
    inverse = 1.0 / (mine[1:2, :] * here + other[1:2, :] * there)
    shift = (mine[2:3, :] * here + other[2:3, :] * there) * inverse
    return here * inverse, shift


def finish_head(t, several, weight, shift, q, kv_head, rows_step, e_in, dp_in, acc, sg_head):
    scale = HEAD ** (-0.5)
    tile = q.shape[0]
    steps = kv_head.shape[0] // rows_step
    first = lax.broadcasted_iota(jnp.int32, (rows_step, PAIR), 1) < HEAD
    zero = jnp.zeros((rows_step, PAIR), jnp.bfloat16)
    out = jnp.zeros((tile, PAIR), jnp.float32)
    for i in range(steps):
        rows = pl.ds(i * rows_step, rows_step)
        probs = e_in[rows, :] * weight
        probs_low = probs.astype(jnp.bfloat16)
        d_scores = (probs * (dp_in[rows, :] - shift) * scale).astype(jnp.bfloat16)
        kv = kv_head[rows, :]
        vk = jnp.concatenate([kv[:, HEAD:], kv[:, :HEAD]], axis=1)
        out = out + dot(probs_low, jnp.where(first, vk, zero), 0, 0)
        out = out + dot(d_scores, jnp.where(first, zero, vk), 0, 0)
        grads = jnp.where(first, dot(d_scores, q, 1, 0), dot(probs_low, q, 1, 0))
        if several:
            grads = jnp.where(t == 0, 0.0, acc[rows, :]) + grads
            acc[rows, :] = grads
        sg_head[rows, :] = grads.astype(jnp.bfloat16)
    return out


def kernel(
    n, heads, tile, step,
    qg, kvs, to, sg,
    qd_all, kv_all, out_all, sg_all, s_scr, dp_scr, acc, parts, stat_mine, stat_other,
    q_send, q_recv, k_send, k_recv, o_send, o_recv, g_send, g_recv, s_send, s_recv, own, own_q,
):
    me = lax.axis_index("section")
    t_rows = qg.shape[0]
    s_rows = kvs.shape[0]
    half = n // 2
    tiles = t_rows * n // tile
    items = heads * tiles
    side = me // half
    base = side * half
    place = lax.rem(me, half)
    twin = lax.rem(me + half, n)
    width = heads * PAIR

    def rows_of(p, rows):
        return pl.ds(pl.multiple_of(p * rows, rows), rows)

    def all_cols(p):
        return pl.ds(pl.multiple_of(lax.rem(p, half) * width, PAIR), width)

    def cols_of(p, h):
        return pl.ds(pl.multiple_of((lax.rem(p, half) * heads + h) * PAIR, PAIR), PAIR)

    def lanes(h):
        return pl.ds(pl.multiple_of(h * PAIR, PAIR), PAIR)

    def push(src, dst, send, recv, p):
        return pltpu.make_async_remote_copy(
            src_ref=src, dst_ref=dst, send_sem=send, recv_sem=recv,
            device_id={"section": p}, device_id_type=pl.DeviceIdType.MESH,
        )

    def q_copy(p, w):
        return push(qg.at[:, all_cols(p)], qd_all.at[rows_of(w, t_rows), :],
                    q_send.at[p], q_recv.at[w], p)

    def k_copy(h, p, w):
        return push(kvs.at[:, cols_of(p, h)], kv_all.at[h, rows_of(lax.rem(w, half), s_rows), :],
                    k_send.at[h, lax.rem(p, half)], k_recv.at[h, lax.rem(w, half)], p)

    def o_copy(h, p, w):
        return push(out_all.at[h, rows_of(p, t_rows), :], parts.at[w // half, :, cols_of(w, h)],
                    o_send.at[h, p], o_recv.at[h, w], p)

    def g_copy(h, p, w):
        return push(sg_all.at[h, rows_of(lax.rem(p, half), s_rows), :], sg.at[:, cols_of(w, h)],
                    g_send.at[h, lax.rem(p, half)], g_recv.at[h, lax.rem(w, half)], p)

    def stat_copy(i):
        return push(stat_mine.at[i], stat_other.at[i], s_send.at[i], s_recv.at[i], twin)

    def own_in(h):
        return pltpu.make_async_copy(
            kvs.at[:, cols_of(me, h)], kv_all.at[h, rows_of(place, s_rows), :], own.at[0, h])

    def own_query():
        return pltpu.make_async_copy(
            qg.at[:, all_cols(me)], qd_all.at[rows_of(me, t_rows), :], own_q.at[0])

    def own_out(h):
        return (
            pltpu.make_async_copy(out_all.at[h, rows_of(me, t_rows), :],
                                  parts.at[side, :, cols_of(me, h)], own.at[1, h]),
            pltpu.make_async_copy(sg_all.at[h, rows_of(place, s_rows), :],
                                  sg.at[:, cols_of(me, h)], own.at[2, h]),
        )

    def each(body):
        @pl.loop(1, n)
        def _(d):
            body(lax.rem(me + d, n))

    def near(body):
        @pl.loop(1, half)
        def _(d):
            body(base + lax.rem(place + d, half))

    barrier = pltpu.get_barrier_semaphore()
    each(lambda p: pl.semaphore_signal(
        barrier, inc=1, device_id={"section": p}, device_id_type=pl.DeviceIdType.MESH))
    own_query().start()

    @pl.loop(0, heads)
    def _(h):
        own_in(h).start()

    pl.semaphore_wait(barrier, n - 1)
    each(lambda p: q_copy(p, me).start())

    @pl.loop(0, heads)
    def _(h):
        near(lambda p: k_copy(h, p, me).start())

    own_query().wait()
    each(lambda p: q_copy(me, p).wait_recv())

    def query(h, t):
        return qd_all[pl.ds(pl.multiple_of(t * tile, tile), tile), lanes(h)]

    @pl.loop(0, items + 1)
    def _(i):
        @pl.when(i < items)
        def _():
            h, t = i // tiles, lax.rem(i, tiles)
            slot = lax.rem(i, 2)

            @pl.when(t == 0)
            def _():
                own_in(h).wait()
                near(lambda p: k_copy(h, me, p).wait_recv())

            scan_scores(query(h, t), kv_all.at[h], step, s_scr.at[slot], dp_scr.at[slot],
                        stat_mine.at[i])
            stat_copy(i).start()

        @pl.when(i > 0)
        def _():
            j = i - 1
            h, t = j // tiles, lax.rem(j, tiles)
            slot = lax.rem(j, 2)
            stat_copy(j).wait_recv()
            weight, shift = merge(stat_mine[j], stat_other[j])
            out_all[h, pl.ds(pl.multiple_of(t * tile, tile), tile), :] = finish_head(
                t, tiles > 1, weight, shift, query(h, t), kv_all.at[h], step,
                s_scr.at[slot], dp_scr.at[slot], acc, sg_all.at[h])

            @pl.when(t == tiles - 1)
            def _():
                near(lambda p: g_copy(h, p, me).start())
                each(lambda p: o_copy(h, p, me).start())
                for c in own_out(h):
                    c.start()

    each(lambda p: q_copy(p, me).wait_send())

    @pl.loop(0, items)
    def _(i):
        stat_copy(i).wait_send()

    @pl.loop(0, heads)
    def _(h):
        for c in own_out(h):
            c.wait()

        def far(p):
            o_copy(h, p, me).wait_send()
            o_copy(h, me, p).wait_recv()
        each(far)

    to[...] = (parts[0] + parts[1]).astype(jnp.bfloat16)

    @pl.loop(0, heads)
    def _(h):
        def close(p):
            k_copy(h, p, me).wait_send()
            g_copy(h, p, me).wait_send()
            g_copy(h, me, p).wait_recv()
        near(close)


def solution(mesh):
    n = mesh.shape["section"]
    half = n // 2

    def per_device(query_grads, key_vals):
        t_rows, columns = query_grads.shape
        s_rows = key_vals.shape[0]
        heads = columns // (PAIR * half)
        targets, sources = t_rows * n, s_rows * half
        tile = math.gcd(targets, 256)
        items = heads * (targets // tile)
        step = max(math.gcd(sources, 256), sources // 8)
        anywhere = pl.BlockSpec(memory_space=pl.ANY)
        dma = pltpu.SemaphoreType.DMA
        return pl.pallas_call(
            functools.partial(kernel, n, heads, tile, step),
            out_shape=(
                jax.ShapeDtypeStruct(query_grads.shape, jnp.bfloat16),
                jax.ShapeDtypeStruct(key_vals.shape, jnp.bfloat16),
            ),
            in_specs=[anywhere, anywhere],
            out_specs=(pl.BlockSpec(memory_space=pltpu.VMEM), anywhere),
            scratch_shapes=[
                pltpu.VMEM((targets, heads * PAIR), jnp.bfloat16),
                pltpu.VMEM((heads, sources, PAIR), jnp.bfloat16),
                pltpu.VMEM((heads, targets, PAIR), jnp.float32),
                pltpu.VMEM((heads, sources, PAIR), jnp.bfloat16),
                pltpu.VMEM((2, sources, tile), jnp.float32),
                pltpu.VMEM((2, sources, tile), jnp.float32),
                pltpu.VMEM((sources if targets > tile else 8, PAIR), jnp.float32),
                pltpu.VMEM((2, t_rows, columns), jnp.float32),
                pltpu.VMEM((items, 8, tile), jnp.float32),
                pltpu.VMEM((items, 8, tile), jnp.float32),
                dma((n,)), dma((n,)),
                dma((heads, half)), dma((heads, half)),
                dma((heads, n)), dma((heads, n)),
                dma((heads, half)), dma((heads, half)),
                dma((items,)), dma((items,)),
                dma((3, heads)), dma((1,)),
            ],
            compiler_params=pltpu.CompilerParams(
                collective_id=0, has_side_effects=True,
                vmem_limit_bytes=48 * 1024 * 1024,
            ),
            cost_estimate=pl.CostEstimate(
                flops=24 * targets * sources * PAIR * heads,
                bytes_accessed=4 * (targets + sources) * heads * PAIR,
                transcendentals=targets * sources * heads,
            ),
            name="exchange_attention",
        )(query_grads, key_vals)

    return jax.shard_map(
        per_device,
        mesh=mesh,
        in_specs=(P(("groups", "section"), None), P(("groups", "section"), None)),
        out_specs=(P(("groups", "section"), None), P(("groups", "section"), None)),
        check_vma=False,
    )
```

time: 117 us -> 92.1 us (0.79)
  the two profiles are of different devices: /device:TPU:13 before, /device:TPU:0 now
where the time goes in v3:
time: 92.1 us; the launch traced here: 91.9 us
  Pallas kernels  86.7 us (94%)
  local copies, waits for them, and re-layouts  4.56 us (5%)
    pallas_call x1, Pallas kernels, per_device(): pl.pallas_call(functools.partial(kernel, n, heads, tile, step), out_shape...  86.7 us
    unnamed x6, local copies, waits for them, and re-layouts  4.56 us

profile of v3, /device:TPU:0, one launch (start us, length us, event | category | flops | bytes accessed | tf_op | source)
XLA Modules:
  0.0 91.9 jit_solution(9004982152832158820)
XLA Ops:
  0.6 0.0 copy-start
  0.6 1.6 %copy-done = bf16[128,8192]{1,0:T(8,128)(2,1)S(1)} copy-done((bf16[128,8192]{1,0:T(8,128)(2,1)S(1)}, bf16[128,8192]{1,0:T(8,128)(2,1)}, u32[]{:S(2)}) %copy-start) | copy-done | bytes 2097176
  2.2 0.0 copy-start.1
  2.2 0.9 %copy-done.1 = bf16[16,8192]{1,0:T(8,128)(2,1)S(1)} copy-done((bf16[16,8192]{1,0:T(8,128)(2,1)S(1)}, bf16[16,8192]{1,0:T(8,128)(2,1)}, u32[]{:S(2)}) %copy-start.1) | copy-done | bytes 262168
  3.2 86.7 %exchange_attention.1 = (bf16[16,8192]{1,0:T(8,128)(2,1)S(1)}, bf16[128,8192]{1,0:T(8,128)(2,1)S(1)}) custom-call(bf16[16,8192]{1,0:T(8,128)(2,1)S(1)} %copy-done.1, bf16[128,8192]{1,0:T(8,128)(2,1)S(1)} %copy-done), custom_call_target="tpu_custom_call" | custom-call | flops 6442450944 | bytes 5242880 | tf_op jit(solution)/shard_map/exchange_attention/pallas_call | solution.py:261
  89.9 0.7 copy.6
  90.6 1.3 %copy.7 = bf16[128,8192]{1,0:T(8,128)(2,1)} copy(bf16[128,8192]{1,0:T(8,128)(2,1)S(1)} %get-tuple-element.5) | data formatting | bytes 4194304
Async XLA Ops:
  0.6 1.6 %copy-start = (bf16[128,8192]{1,0:T(8,128)(2,1)S(1)}, bf16[128,8192]{1,0:T(8,128)(2,1)}, u32[]{:S(2)}) copy-start(bf16[128,8192]{1,0:T(8,128)(2,1)} %kvs.1) | copy-start | bytes 6291460
  2.2 0.9 %copy-start.1 = (bf16[16,8192]{1,0:T(8,128)(2,1)S(1)}, bf16[16,8192]{1,0:T(8,128)(2,1)}, u32[]{:S(2)}) copy-start(bf16[16,8192]{1,0:T(8,128)(2,1)} %qg.1) | copy-start | bytes 786436

commit v4 on v3

--- a/solution.py
+++ b/solution.py
@@ -212,8 +212,8 @@
 
             @pl.when(t == tiles - 1)
             def _():
+                each(lambda p: o_copy(h, p, me).start())
                 near(lambda p: g_copy(h, p, me).start())
-                each(lambda p: o_copy(h, p, me).start())
                 for c in own_out(h):
                     c.start()
 

time: 92.1 us -> 90.1 us (0.978)
  Pallas kernels: 86.7 us -> 84.7 us
    pallas_call x1, Pallas kernels: 86.7 us -> 84.7 us  [per_device(): pl.pallas_call(functools.partial(kernel, n, heads, tile, step), out_shape...]
where the time goes in v4:
time: 90.1 us; the launch traced here: 89.9 us
  Pallas kernels  84.7 us (94%)
  local copies, waits for them, and re-layouts  4.56 us (5%)
    pallas_call x1, Pallas kernels, per_device(): pl.pallas_call(functools.partial(kernel, n, heads, tile, step), out_shape...  84.7 us
    unnamed x6, local copies, waits for them, and re-layouts  4.56 us

profile of v4, /device:TPU:0, one launch (start us, length us, event | category | flops | bytes accessed | tf_op | source)
XLA Modules:
  0.0 89.9 jit_solution(7551956091169776168)
XLA Ops:
  0.6 0.0 copy-start
  0.6 1.6 %copy-done = bf16[128,8192]{1,0:T(8,128)(2,1)S(1)} copy-done((bf16[128,8192]{1,0:T(8,128)(2,1)S(1)}, bf16[128,8192]{1,0:T(8,128)(2,1)}, u32[]{:S(2)}) %copy-start) | copy-done | bytes 2097176
  2.2 0.0 copy-start.1
  2.2 0.9 %copy-done.1 = bf16[16,8192]{1,0:T(8,128)(2,1)S(1)} copy-done((bf16[16,8192]{1,0:T(8,128)(2,1)S(1)}, bf16[16,8192]{1,0:T(8,128)(2,1)}, u32[]{:S(2)}) %copy-start.1) | copy-done | bytes 262168
  3.2 84.7 %exchange_attention.1 = (bf16[16,8192]{1,0:T(8,128)(2,1)S(1)}, bf16[128,8192]{1,0:T(8,128)(2,1)S(1)}) custom-call(bf16[16,8192]{1,0:T(8,128)(2,1)S(1)} %copy-done.1, bf16[128,8192]{1,0:T(8,128)(2,1)S(1)} %copy-done), custom_call_target="tpu_custom_call" | custom-call | flops 6442450944 | bytes 5242880 | tf_op jit(solution)/shard_map/exchange_attention/pallas_call | solution.py:261
  87.9 0.7 copy.6
  88.6 1.3 %copy.7 = bf16[128,8192]{1,0:T(8,128)(2,1)} copy(bf16[128,8192]{1,0:T(8,128)(2,1)S(1)} %get-tuple-element.5) | data formatting | bytes 4194304
Async XLA Ops:
  0.6 1.6 %copy-start = (bf16[128,8192]{1,0:T(8,128)(2,1)S(1)}, bf16[128,8192]{1,0:T(8,128)(2,1)}, u32[]{:S(2)}) copy-start(bf16[128,8192]{1,0:T(8,128)(2,1)} %kvs.1) | copy-start | bytes 6291460
  2.2 0.9 %copy-start.1 = (bf16[16,8192]{1,0:T(8,128)(2,1)S(1)}, bf16[16,8192]{1,0:T(8,128)(2,1)}, u32[]{:S(2)}) copy-start(bf16[16,8192]{1,0:T(8,128)(2,1)} %qg.1) | copy-start | bytes 786436
